TPU v7x, 32 devices: a whole 2x2x4 slice. The times are simulated.
32 devices in a mesh: dom: 8 (over z, y), sub: 4 (over x, core).
Axes of the slice: x: 2, y: 2, z: 4, core: 2. Of those that a mesh axis runs over, the one named last changes fastest.
Arguments:
- leaf_hist: float32 [112, 65536], P(None, ('dom', 'sub')), may hold values from -6 to 6
- leaf_weight: float32 [65536], P(('dom', 'sub')), may hold values from 0.1 to 1
- leaf_parent: int32 [65536], P(('dom', 'sub')), may hold values from 0 to 2047, as said below
- entry_parent: int32 [16384], P(('dom', 'sub')), may hold values from 0 to 511
- entry_dest: int32 [16384, 1], P(('dom', 'sub')), may hold values from 0 to 7; in each aligned block of 512 rows (0 to 511, 512 to 1023, ...) at most 256 rows name the same one
- entry_crash: int32 [16384], P(('dom', 'sub')), may hold values from 0 to 511
- entry_weight: float32 [16384], P(('dom', 'sub')), may hold values from 0.05 to 1
Outputs:
- crash_hist: float32 [80, 16384], P(None, ('dom', 'sub'))
Inputs may be any that keep to these rules, and one draw needn't show every extreme that they name: `leaf_parent`: a leaf's parent is numbered 0 to 2047 within the leaves of its index of dom; every parent has at least one leaf. `entry_dest`: among the 512 entries of one device no index of dom is named more than 256 times.
All inputs are finite; a program needn't handle non-finite values.
Results may differ from a plain program's by a relative error of at most 0.00011.
Values sent between devices are 32-bit elements; how exact they have to be, the bound alone decides.
A program may use at most 64 MiB of HBM per device.

v0:
```python
import jax
import jax.numpy as jnp
from jax import lax
from jax.sharding import PartitionSpec as P

HIST = 16
THICK = 7
CTHICK = 5
PAR_DEV = 512
ENT_DEV = 512
CRASH_DEV = 512


def remap_table():
    target = jnp.arange(CTHICK, dtype=jnp.float32) * ((THICK - 1) / (CTHICK - 1))
    source = jnp.arange(THICK, dtype=jnp.float32)
    return jnp.maximum(0.0, 1.0 - jnp.abs(target[:, None] - source[None, :]))


def remap_rows(values):
    columns = values.shape[1]
    cube = values.reshape(HIST, THICK, columns)
    result = jnp.einsum("ct,htn->hcn", remap_table(), cube, precision=lax.Precision.HIGHEST)
    return result.reshape(HIST * CTHICK, columns)


def per_device(
    leaf_hist, leaf_weight, leaf_parent, entry_parent, entry_dest, entry_crash, entry_weight
):
    sub_total = lax.axis_size("sub")
    dom_total = lax.axis_size("dom")
    group_parents = PAR_DEV * sub_total
    weighted = (leaf_hist * leaf_weight[None, :]).T
    partial_sums = jax.ops.segment_sum(weighted, leaf_parent, num_segments=group_parents).T
    partial_weight = jax.ops.segment_sum(leaf_weight, leaf_parent, num_segments=group_parents)
    parent_sums, parent_weight = (
        lax.psum_scatter(partial_sums, "sub", scatter_dimension=1, tiled=True),
        lax.psum_scatter(partial_weight, "sub", scatter_dimension=0, tiled=True),
    )
    parent_hist = parent_sums / parent_weight[None, :]
    parent_hist = remap_rows(parent_hist)
    capacity = max(2, 4 * ENT_DEV // dom_total)
    slot_total = dom_total * capacity
    destination = entry_dest[:, 0]
    entry_total = destination.shape[0]
    ordering = jnp.argsort(destination, stable=True)
    sorted_destination = destination[ordering]
    first_slot = jnp.searchsorted(sorted_destination, sorted_destination, side="left")
    positions = jnp.arange(entry_total, dtype=jnp.int32)
    slot_sorted = sorted_destination * capacity + (positions - first_slot)
    slot_index = jnp.zeros((entry_total,), jnp.int32).at[ordering].set(slot_sorted)
    carried = jnp.take(parent_hist, entry_parent, axis=1) * entry_weight[None, :]
    send_values = (
        jnp.zeros((carried.shape[0], slot_total), jnp.float32).at[:, slot_index].set(carried)
    )
    send_weight = jnp.zeros((1, slot_total), jnp.float32).at[0, slot_index].set(entry_weight)
    send_crash = jnp.zeros((1, slot_total), jnp.int32).at[0, slot_index].set(entry_crash)
    got_values, got_weight, got_crash = (
        lax.all_to_all(send_values, "dom", split_axis=1, concat_axis=1, tiled=True),
        lax.all_to_all(send_weight, "dom", split_axis=1, concat_axis=1, tiled=True),
        lax.all_to_all(send_crash, "dom", split_axis=1, concat_axis=1, tiled=True),
    )
    crash_sums = jax.ops.segment_sum(got_values.T, got_crash[0], num_segments=CRASH_DEV).T
    crash_weight = jax.ops.segment_sum(got_weight[0], got_crash[0], num_segments=CRASH_DEV)
    return crash_sums / jnp.maximum(crash_weight, 1.0)[None, :]


def solution(mesh):
    in_specs = (
        P(None, ("dom", "sub")),
        P(("dom", "sub")),
        P(("dom", "sub")),
        P(("dom", "sub")),
        P(("dom", "sub"), None),
        P(("dom", "sub")),
        P(("dom", "sub")),
    )
    out_specs = P(None, ("dom", "sub"))
    return jax.shard_map(
        per_device, mesh=mesh, in_specs=in_specs, out_specs=out_specs, check_vma=False
    )
```

profile of v0, /device:TPU:0, one launch (start us, length us, event | category | flops | bytes accessed | tf_op | source)
XLA Modules:
  0.0 158.5 jit_solution(16172167199306809361)
XLA Ops:
  8.1 11.8 %scatter_custom_fusion.2 = f32[2048,112]{1,0:T(8,128)S(1)} fusion(s32[2048]{0:T(1024)} %param.11, f32[2048,112]{1,0:T(8,128)S(1)} %copy.28, f32[]{:T(128)} %constant.59.clone.1), kind=kCustom, calls=%fused_computation.17 | custom fusion | flops 229376 | bytes 918016 | tf_op jit(solution)/shard_map/scatter-add | solution.py:34
  22.0 3.8 %sort.17 = (s32[512]{0:T(512)}, s32[512]{0:T(512)S(1)}) sort(s32[512]{0:T(512)S(1)} %bitcast.22, s32[512]{0:T(512)S(1)} %iota.16), dimensions={0}, to_apply=%region_0.0 | sort | flops 4608 | bytes 8192 | tf_op jit(solution)/shard_map/jit(argsort)/sort | solution.py:46
  25.8 3.5 %gather_fusion.1 = s32[512]{0:T(512)S(1)} fusion(s32[512]{0:T(512)S(1)} %bitcast.23, s32[1024]{0:T(1024)S(1)} %pad_clamp_fusion.2), kind=kCustom, calls=%fused_computation.1 | custom fusion | bytes 6144 | tf_op jit(solution)/shard_map/gather | solution.py:47
  29.3 35.9 %while.25 = (s32[]{:T(128)}, u32[512]{0:T(512)S(1)}, u32[512]{0:T(512)S(1)}, s32[512]{0:T(512)S(1)}, s32[]{:T(128)}, /*index=5*/s32[]{:T(128)}, s32[]{}) while((s32[]{:T(128)}, u32[512]{0:T(512)S(1)}, u32[512]{0:T(512)S(1)}, s32[512]{0:T(512)S(1)}, s32[]{:T(128)}, /*index=5*/s32[]{:T(128)}, s32[]{}) %tuple.36), condition=%wide.region_2.0_spmd.clone, body=%wide.region_1.0_spmd.clone.sunk | while | flops 10244 | bytes 40037 | solution.py:48
  29.3 3.5 %gather_fusion = s32[512]{0:T(512)S(1)} fusion(s32[512]{0:T(512)S(1)} %get-tuple-element.146, u32[1024]{0:T(1024)S(1)} %pad_clamp_fusion.4), kind=kCustom, calls=%fused_computation.clone.clone.1 | custom fusion | bytes 6144 | tf_op jit(solution)/shard_map/jit(searchsorted)/jit(_searchsorted_scan_impl)/vmap(jit(_searchsorted_scan_impl))/while/body/eval_jaxpr/gather | solution.py:48
  32.9 3.5 %gather_fusion = s32[512]{0:T(512)S(1)} fusion(s32[512]{0:T(512)S(1)} %get-tuple-element.146, u32[1024]{0:T(1024)S(1)} %pad_clamp_fusion.4), kind=kCustom, calls=%fused_computation.clone.clone.1 | custom fusion | bytes 6144 | tf_op jit(solution)/shard_map/jit(searchsorted)/jit(_searchsorted_scan_impl)/vmap(jit(_searchsorted_scan_impl))/while/body/eval_jaxpr/gather | solution.py:48
  36.5 3.5 %gather_fusion = s32[512]{0:T(512)S(1)} fusion(s32[512]{0:T(512)S(1)} %get-tuple-element.146, u32[1024]{0:T(1024)S(1)} %pad_clamp_fusion.4), kind=kCustom, calls=%fused_computation.clone.clone.1 | custom fusion | bytes 6144 | tf_op jit(solution)/shard_map/jit(searchsorted)/jit(_searchsorted_scan_impl)/vmap(jit(_searchsorted_scan_impl))/while/body/eval_jaxpr/gather | solution.py:48
  40.1 3.5 %gather_fusion = s32[512]{0:T(512)S(1)} fusion(s32[512]{0:T(512)S(1)} %get-tuple-element.146, u32[1024]{0:T(1024)S(1)} %pad_clamp_fusion.4), kind=kCustom, calls=%fused_computation.clone.clone.1 | custom fusion | bytes 6144 | tf_op jit(solution)/shard_map/jit(searchsorted)/jit(_searchsorted_scan_impl)/vmap(jit(_searchsorted_scan_impl))/while/body/eval_jaxpr/gather | solution.py:48
  43.7 3.5 %gather_fusion = s32[512]{0:T(512)S(1)} fusion(s32[512]{0:T(512)S(1)} %get-tuple-element.146, u32[1024]{0:T(1024)S(1)} %pad_clamp_fusion.4), kind=kCustom, calls=%fused_computation.clone.clone.1 | custom fusion | bytes 6144 | tf_op jit(solution)/shard_map/jit(searchsorted)/jit(_searchsorted_scan_impl)/vmap(jit(_searchsorted_scan_impl))/while/body/eval_jaxpr/gather | solution.py:48
  47.3 3.5 %gather_fusion = s32[512]{0:T(512)S(1)} fusion(s32[512]{0:T(512)S(1)} %get-tuple-element.146, u32[1024]{0:T(1024)S(1)} %pad_clamp_fusion.4), kind=kCustom, calls=%fused_computation.clone.clone.1 | custom fusion | bytes 6144 | tf_op jit(solution)/shard_map/jit(searchsorted)/jit(_searchsorted_scan_impl)/vmap(jit(_searchsorted_scan_impl))/while/body/eval_jaxpr/gather | solution.py:48
  50.8 3.5 %gather_fusion = s32[512]{0:T(512)S(1)} fusion(s32[512]{0:T(512)S(1)} %get-tuple-element.146, u32[1024]{0:T(1024)S(1)} %pad_clamp_fusion.4), kind=kCustom, calls=%fused_computation.clone.clone.1 | custom fusion | bytes 6144 | tf_op jit(solution)/shard_map/jit(searchsorted)/jit(_searchsorted_scan_impl)/vmap(jit(_searchsorted_scan_impl))/while/body/eval_jaxpr/gather | solution.py:48
  54.4 3.5 %gather_fusion = s32[512]{0:T(512)S(1)} fusion(s32[512]{0:T(512)S(1)} %get-tuple-element.146, u32[1024]{0:T(1024)S(1)} %pad_clamp_fusion.4), kind=kCustom, calls=%fused_computation.clone.clone.1 | custom fusion | bytes 6144 | tf_op jit(solution)/shard_map/jit(searchsorted)/jit(_searchsorted_scan_impl)/vmap(jit(_searchsorted_scan_impl))/while/body/eval_jaxpr/gather | solution.py:48
  58.0 3.5 %gather_fusion = s32[512]{0:T(512)S(1)} fusion(s32[512]{0:T(512)S(1)} %get-tuple-element.146, u32[1024]{0:T(1024)S(1)} %pad_clamp_fusion.4), kind=kCustom, calls=%fused_computation.clone.clone.1 | custom fusion | bytes 6144 | tf_op jit(solution)/shard_map/jit(searchsorted)/jit(_searchsorted_scan_impl)/vmap(jit(_searchsorted_scan_impl))/while/body/eval_jaxpr/gather | solution.py:48
  61.6 3.5 %gather_fusion = s32[512]{0:T(512)S(1)} fusion(s32[512]{0:T(512)S(1)} %get-tuple-element.146, u32[1024]{0:T(1024)S(1)} %pad_clamp_fusion.4), kind=kCustom, calls=%fused_computation.clone.clone.1 | custom fusion | bytes 6144 | tf_op jit(solution)/shard_map/jit(searchsorted)/jit(_searchsorted_scan_impl)/vmap(jit(_searchsorted_scan_impl))/while/body/eval_jaxpr/gather | solution.py:48
  67.6 3.2 %scatter_custom_fusion.1 = s32[2048]{0:T(1024)} fusion(s32[512]{0:T(512)S(1)} %compare_select_fusion.1, s32[512]{0:T(512)} %param.14, s32[]{:T(128)} %constant.60.clone.1), kind=kCustom, calls=%fused_computation.36 | custom fusion | bytes 8704 | tf_op jit(solution)/shard_map/scatter | solution.py:57
  70.8 7.3 %all-to-all-start = ((s32[1,8,256]{2,0,1:T(1,128)}), s32[1,8,256]{2,0,1:T(1,128)S(1)}, u32[]{:S(2)}, u32[]{:S(2)}) async-start(s32[1,8,256]{2,0,1:T(1,128)} %bitcast.1), calls=%async_computation | async-start | bytes 16384 | tf_op jit(solution)/shard_map/all_to_all | solution.py:61
  78.1 12.2 %scatter_custom_fusion.3 = f32[2048]{0:T(1024)S(1)} fusion(s32[2048]{0:T(1024)} %param.11, f32[2048]{0:T(1024)} %param.10, f32[]{:T(128)} %constant.59.clone.1), kind=kCustom, calls=%fused_computation.45 | custom fusion | flops 2048 | bytes 8704 | tf_op jit(solution)/shard_map/scatter-add | solution.py:35
  91.0 3.0 %scatter_custom_fusion.6 = f32[2048]{0:T(1024)} fusion(s32[512]{0:T(512)S(1)} %compare_select_fusion.1, f32[512]{0:T(512)S(1)} %copy-done.2, f32[]{:T(128)} %constant.59.clone.1), kind=kCustom, calls=%fused_computation.43 | custom fusion | bytes 8196 | tf_op jit(solution)/shard_map/scatter | solution.py:56
  95.9 6.3 %all-reduce.1 = f32[2048]{0:T(1024)S(1)} all-reduce(f32[2048]{0:T(1024)S(1)} %scatter_custom_fusion.3), channel_id=3, replica_groups=mesh['dom'=8,'sub'=4] {'sub'}, use_global_device_ids=true, to_apply=%region_8.9.clone | all-reduce | flops 2048 | bytes 16384
  103.4 5.5 %all-to-all-start.2 = ((f32[1,8,256]{2,0,1:T(1,128)}), f32[1,8,256]{2,0,1:T(1,128)S(1)}, u32[]{:S(2)}, u32[]{:S(2)}) async-start(f32[1,8,256]{2,0,1:T(1,128)} %bitcast.9), calls=%async_computation.3 | async-start | bytes 16384 | tf_op jit(solution)/shard_map/all_to_all | solution.py:60
  109.6 3.1 %scatter_custom_fusion.4 = f32[80,2048]{0,1:T(8,128)S(1)} fusion(s32[512]{0:T(512)S(1)} %compare_select_fusion.1, f32[]{:T(128)} %constant.59.clone.1, f32[512]{0:T(512)S(1)} %copy-done.2, f32[]{:T(128)} %constant.69.clone.1, pred[512]{0:T(512)(128)(4,1)S(1)} %compare_and_fusion, f32[80,512]{0,1:T(8,128)S(1)} %copy.30, s32[1024]{0:T(1024)S(1)} %pad_clamp_fusion.1), kind=kCustom, calls=%fused_computation.19 | custom fusion | flops 81920 | bytes 924168 | tf_op jit(solution)/shard_map/scatter | solution.py:54
  115.5 4.3 %all-to-all-start.1 = ((f32[80,8,256]{2,0,1:T(8,128)}), f32[80,8,256]{2,0,1:T(8,128)S(1)}, u32[]{:S(2)}, u32[]{:S(2)}) async-start(f32[80,8,256]{2,0,1:T(8,128)} %copy.31), calls=%async_computation.2 | async-start | bytes 1310720 | tf_op jit(solution)/shard_map/all_to_all | solution.py:59
  119.8 14.7 %scatter_custom_fusion.7 = f32[512]{0:T(512)S(1)} fusion(s32[2048]{0:T(1024)S(1)} %bitcast.28, f32[2048]{0:T(1024)S(1)} %bitcast.30, f32[]{:T(128)} %constant.59.clone.1), kind=kCustom, calls=%fused_computation.53 | custom fusion | flops 2048 | bytes 2052 | tf_op jit(solution)/shard_map/scatter-add | solution.py:64
  136.8 13.8 %scatter_custom_fusion.5 = f32[512,80]{1,0:T(8,128)S(1)} fusion(s32[2048]{0:T(1024)S(1)} %bitcast.29, f32[2048,80]{1,0:T(8,128)S(1)} %copy.33, f32[]{:T(128)} %constant.59.clone.1), kind=kCustom, calls=%fused_computation.26 | custom fusion | flops 163840 | bytes 163844 | tf_op jit(solution)/shard_map/scatter-add | solution.py:63
  (92 shorter events, 16.1 us)
Async XLA Ops:
  6.5 95.9 %reduce-scatter.2.cloned.1.call-start = ((), (), s32[]{:S(2)}) async-start(), calls=%async_computation.4 | async-start | bytes 1146880 | tf_op jit(solution)/shard_map/reduce_scatter | solution.py:37
  21.3 0.7 copy-start
  29.3 73.1 %copy-start.1 = (s32[512]{0:T(512)S(1)}, s32[512]{0:T(512)}, u32[]{:S(2)}) copy-start(s32[512]{0:T(512)} %param.12) | copy-start | bytes 6148
  70.8 32.6 %all-to-all-start = ((s32[1,8,256]{2,0,1:T(1,128)}), s32[1,8,256]{2,0,1:T(1,128)S(1)}, u32[]{:S(2)}, u32[]{:S(2)}) async-start(s32[1,8,256]{2,0,1:T(1,128)} %bitcast.1), calls=%async_computation | async-start | bytes 16384 | tf_op jit(solution)/shard_map/all_to_all | solution.py:61
  90.3 0.7 copy-start.2
  94.0 0.7 copy-start.3
  103.4 12.0 %all-to-all-start.2 = ((f32[1,8,256]{2,0,1:T(1,128)}), f32[1,8,256]{2,0,1:T(1,128)S(1)}, u32[]{:S(2)}, u32[]{:S(2)}) async-start(f32[1,8,256]{2,0,1:T(1,128)} %bitcast.9), calls=%async_computation.3 | async-start | bytes 16384 | tf_op jit(solution)/shard_map/all_to_all | solution.py:60
  115.5 20.9 %all-to-all-start.1 = ((f32[80,8,256]{2,0,1:T(8,128)}), f32[80,8,256]{2,0,1:T(8,128)S(1)}, u32[]{:S(2)}, u32[]{:S(2)}) async-start(f32[80,8,256]{2,0,1:T(8,128)} %copy.31), calls=%async_computation.2 | async-start | bytes 1310720 | tf_op jit(solution)/shard_map/all_to_all | solution.py:59
Sparse Core Ops, SparseCore 0:
  21.4 26.7 reduce-scatter.1
where the time goes:
time: 158 us
  other arithmetic  62.3 us (39%)
  local copies, waits for them, and re-layouts  53.8 us (34%)
  starting transfers between devices  17.2 us (11%)
  between operations  14.3 us (9%)
  blocking collectives  6.35 us (4%)
  waiting for transfers between devices  3.61 us (2%)
    gather x10, local copies, waits for them, and re-layouts, per_device(): jnp.searchsorted(sorted_destination, sorted_destination, side='left')  34.9 us
    scatter-add x1, other arithmetic, per_device(): jax.ops.segment_sum(got_weight[0], got_crash[0], num_segments=CRASH_DEV)  14.7 us
    scatter-add x1, other arithmetic, per_device(): jax.ops.segment_sum(got_values.T, got_crash[0], num_segments=CRASH_DEV)  13.8 us
    scatter-add x1, other arithmetic, per_device(): jax.ops.segment_sum(leaf_weight, leaf_parent, num_segments=group_parents)  12.2 us
    scatter-add x1, other arithmetic, per_device(): jax.ops.segment_sum(weighted, leaf_parent, num_segments=group_parents)  11.8 us
    all_to_all x1, starting transfers between devices, per_device(): lax.all_to_all(send_crash, 'dom', split_axis=1, concat_axis=1, tiled=True)  7.28 us
    unnamed x1, blocking collectives  6.35 us
    all_to_all x1, starting transfers between devices, per_device(): lax.all_to_all(send_weight, 'dom', split_axis=1, concat_axis=1, tiled=True)  5.53 us
  transfers between devices with their start and end apart: 4, of which 2 were waited for; matrix products, arithmetic and copies ran while one was open for 53% of the time, Pallas kernels for 0%

commit v1 on v0

--- a/solution.py
+++ b/solution.py
@@ -1,6 +1,10 @@
+import functools
+
 import jax
 import jax.numpy as jnp
 from jax import lax
+from jax.experimental import pallas as pl
+from jax.experimental.pallas import tpu as pltpu
 from jax.sharding import PartitionSpec as P
 
 HIST = 16
@@ -65,7 +69,251 @@
     return crash_sums / jnp.maximum(crash_weight, 1.0)[None, :]
 
 
+MESH = pl.DeviceIdType.MESH
+F32, BF16, I32 = jnp.float32, jnp.bfloat16, jnp.int32
+HEAD = 8
+ROWS = HIST * CTHICK
+CHUNKS = 2
+
+
+def dot_nn(a, b):
+    return lax.dot_general(a, b, (((1,), (0,)), ((), ())), preferred_element_type=F32)
+
+
+def dot_nt(a, b):
+    return lax.dot_general(a, b, (((1,), (1,)), ((), ())), preferred_element_type=F32)
+
+
+def terms(x, count):
+    parts = []
+    for _ in range(count):
+        part = x.astype(BF16).astype(F32)
+        parts.append(part)
+        x = x - part
+    return jnp.concatenate(parts, axis=0).astype(BF16)
+
+
+def fold(x, count):
+    rows = x.shape[0] // count
+    total = x[:rows]
+    for i in range(1, count):
+        total = total + x[i * rows : (i + 1) * rows]
+    return total
+
+
+def one_hot(index_row, rows):
+    step = min(rows, 256)
+    count = index_row.shape[1]
+    iota = lax.broadcasted_iota(I32, (step, count), 0).astype(F32).astype(BF16)
+    one, zero = jnp.ones((), BF16), jnp.zeros((), BF16)
+    blocks = []
+    for base in range(0, rows, step):
+        low = index_row - base
+        low = jnp.where((low >= 0) & (low < step), low, -1).astype(F32).astype(BF16)
+        blocks.append(jnp.where(iota == low, one, zero))
+    return jnp.concatenate(blocks, axis=0) if len(blocks) > 1 else blocks[0]
+
+
+def remap_matrix():
+    row = lax.broadcasted_iota(I32, (ROWS, HIST * THICK), 0)
+    column = lax.broadcasted_iota(I32, (ROWS, HIST * THICK), 1)
+    row_h = (row * 205) >> 10
+    column_h = (column * 147) >> 10
+    target = (row - row_h * CTHICK).astype(F32) * ((THICK - 1) / (CTHICK - 1))
+    source = (column - column_h * THICK).astype(F32)
+    weight = jnp.maximum(0.0, 1.0 - jnp.abs(target - source))
+    return jnp.where(row_h == column_h, weight, 0.0).astype(BF16)
+
+
+def fused_kernel(
+    n_dom, capacity,
+    hist_hbm, leaf_weight, leaf_parent, entry_parent, entry_dest, entry_crash, entry_weight,
+    out_ref,
+    hist, data, kept, core_send, core_recv, x_send, x_recv, meta, meta_recv, pick, drop, pay, pay_recv, total,
+    hist_sem, core_ssem, core_rsem, x_ssem, x_rsem, meta_ssem, meta_rsem, pay_ssem, pay_rsem,
+):
+    dom, sub = lax.axis_index("dom"), lax.axis_index("sub")
+    load = pltpu.make_async_copy(hist_hbm, hist, hist_sem)
+    load.start()
+    core = lax.rem(sub, 2)
+    x = sub // 2
+    core_peer = (dom, x * 2 + 1 - core)
+    x_peer = (dom, (1 - x) * 2 + core)
+
+    def dom_of(mask):
+        peer = jnp.zeros((), I32)
+        bit = 1
+        while bit < n_dom:
+            own = lax.rem(dom // bit, 2)
+            peer = peer + bit * (1 - own if mask & bit else own)
+            bit *= 2
+        return peer
+
+    dom_peers = [(dom_of(mask), sub) for mask in range(n_dom)]
+    barrier = pltpu.get_barrier_semaphore()
+    for peer in [core_peer, x_peer] + dom_peers[1:]:
+        pl.semaphore_signal(barrier, inc=1, device_id=peer, device_id_type=MESH)
+
+    def remote(source, target, ssem, rsem, peer):
+        return pltpu.make_async_remote_copy(
+            src_ref=source, dst_ref=target, send_sem=ssem, recv_sem=rsem, device_id=peer, device_id_type=MESH
+        )
+
+    load.wait()
+    high = hist[...].astype(BF16)
+    low = (hist[...] - high.astype(F32)).astype(BF16)
+    table = remap_matrix()
+    remapped = dot_nn(table, high) + dot_nn(table, low)
+    weight = leaf_weight[...]
+    first = lax.broadcasted_iota(I32, (HEAD, weight.shape[1]), 0) == 0
+    head = jnp.where(first, weight, 0.0)
+    data[...] = terms(jnp.concatenate([head, remapped * weight], axis=0), 2)
+
+    def quarter(index):
+        return fold(dot_nt(data[...], one_hot(leaf_parent[...] - index * PAR_DEV, PAR_DEV)), 2)
+
+    core_copies = [
+        remote(core_send.at[i], core_recv.at[i], core_ssem.at[i], core_rsem.at[i], core_peer) for i in range(2)
+    ]
+    bounds = [0] + [HEAD + ROWS * (c + 1) // CHUNKS for c in range(CHUNKS)]
+    spans = [pl.ds(bounds[c], bounds[c + 1] - bounds[c]) for c in range(CHUNKS)]
+    x_copies = [
+        remote(x_send.at[span], x_recv.at[span], x_ssem.at[c], x_rsem.at[c], x_peer) for c, span in enumerate(spans)
+    ]
+    core_send[0] = quarter((1 - x) * 2 + 1 - core)
+    pl.semaphore_wait(barrier, n_dom + 1)
+    core_copies[0].start()
+    kept[0] = quarter((1 - x) * 2 + core)
+    core_copies[0].wait_recv()
+    for c, span in enumerate(spans):
+        x_send[span] = kept[0, span] + core_recv[0, span]
+        x_copies[c].start()
+    core_send[1] = quarter(x * 2 + 1 - core)
+    core_copies[1].start()
+    kept[1] = quarter(x * 2 + core)
+
+    entries = entry_parent.shape[1]
+    named = entry_dest[...]
+    mask = jnp.zeros_like(named)
+    bit = 1
+    while bit < n_dom:
+        own = lax.rem(dom // bit, 2)
+        part = lax.rem(named // bit, 2)
+        mask = mask + bit * jnp.abs(part - own)
+        bit *= 2
+    padded = max(n_dom, 8)
+    is_dest = (lax.broadcasted_iota(I32, (padded, entries), 0) == mask).astype(F32)
+    earlier = lax.broadcasted_iota(I32, (entries, entries), 0) < lax.broadcasted_iota(I32, (entries, entries), 1)
+    before = dot_nn(is_dest.astype(BF16), earlier.astype(F32).astype(BF16))
+    rank = jnp.sum(before * is_dest, axis=0, keepdims=True).astype(I32)
+    slot = mask * capacity + rank
+    rows = jnp.concatenate(
+        [
+            entry_weight[...],
+            entry_crash[...].astype(F32),
+            entry_parent[...].astype(F32),
+            jnp.zeros((5, entries), F32),
+        ],
+        axis=0,
+    )
+    rows = terms(rows, 3)
+    for m in range(n_dom):
+        meta[m] = fold(dot_nt(rows, one_hot(slot - m * capacity, capacity)), 3)
+    meta_copies = {
+        m: remote(meta.at[m], meta_recv.at[m], meta_ssem.at[m], meta_rsem.at[m], dom_peers[m])
+        for m in range(1, n_dom)
+    }
+    for copy in meta_copies.values():
+        copy.start()
+    for m in range(n_dom):
+        pick[m] = one_hot(meta[m, 2:3].astype(I32), PAR_DEV)
+
+    core_copies[1].wait_recv()
+    pay_copies = {}
+    inverse = None
+    for c, span in enumerate(spans):
+        x_copies[c].wait_recv()
+        sums = kept[1, span] + core_recv[1, span] + x_recv[span]
+        if c == 0:
+            inverse = 1.0 / sums[:1]
+            sums = sums[HEAD:]
+        means = terms(sums * inverse, 2)
+        for m in list(range(n_dom - 1, -1, -1)):
+            pay[c, m] = fold(dot_nn(means, pick[m]), 2) * meta[m, :1]
+            if m:
+                copy = remote(pay.at[c, m], pay_recv.at[c, m], pay_ssem.at[c, m], pay_rsem.at[c, m], dom_peers[m])
+                copy.start()
+                pay_copies[c, m] = copy
+
+    crash_weight = jnp.zeros((1, CRASH_DEV), F32)
+    for m in range(n_dom):
+        if m:
+            meta_copies[m].wait_recv()
+        got = meta_recv[m] if m else meta[0]
+        drop[m] = one_hot(got[1:2].astype(I32), CRASH_DEV)
+        crash_weight = crash_weight + fold(dot_nt(terms(got, 3), drop[m]), 3)[:1]
+    inverse = 1.0 / jnp.maximum(crash_weight, 1.0)
+    size = ROWS // CHUNKS
+    for c in range(CHUNKS):
+        total[...] = dot_nt(terms(pay[c, 0], 2), drop[0])
+        for m in list(range(n_dom - 1, 0, -1)):
+            pay_copies[c, m].wait_recv()
+            total[...] += dot_nt(terms(pay_recv[c, m], 2), drop[m])
+        out_ref[pl.ds(c * size, size)] = fold(total[...], 2) * inverse
+    for copy in core_copies + x_copies + list(meta_copies.values()) + list(pay_copies.values()):
+        copy.wait_send()
+
+
+def fused(leaf_hist, leaf_weight, leaf_parent, entry_parent, entry_dest, entry_crash, entry_weight):
+    n_dom = lax.axis_size("dom")
+    capacity = 4 * ENT_DEV // n_dom
+    leaves = leaf_hist.shape[1]
+    size = ROWS // CHUNKS
+    vmem = pl.BlockSpec(memory_space=pltpu.VMEM)
+    dma = pltpu.SemaphoreType.DMA
+    row = lambda array: array.reshape(1, -1)
+    return pl.pallas_call(
+        functools.partial(fused_kernel, n_dom, capacity),
+        out_shape=jax.ShapeDtypeStruct((ROWS, CRASH_DEV), F32),
+        in_specs=[pl.BlockSpec(memory_space=pl.ANY)] + [vmem] * 6,
+        out_specs=vmem,
+        scratch_shapes=[
+            pltpu.VMEM((HIST * THICK, leaves), F32),
+            pltpu.VMEM((2 * (HEAD + ROWS), leaves), BF16),
+            pltpu.VMEM((2, HEAD + ROWS, PAR_DEV), F32),
+            pltpu.VMEM((2, HEAD + ROWS, PAR_DEV), F32),
+            pltpu.VMEM((2, HEAD + ROWS, PAR_DEV), F32),
+            pltpu.VMEM((HEAD + ROWS, PAR_DEV), F32),
+            pltpu.VMEM((HEAD + ROWS, PAR_DEV), F32),
+            pltpu.VMEM((n_dom, 8, capacity), F32),
+            pltpu.VMEM((n_dom, 8, capacity), F32),
+            pltpu.VMEM((n_dom, PAR_DEV, capacity), BF16),
+            pltpu.VMEM((n_dom, CRASH_DEV, capacity), BF16),
+            pltpu.VMEM((CHUNKS, n_dom, size, capacity), F32),
+            pltpu.VMEM((CHUNKS, n_dom, size, capacity), F32),
+            pltpu.VMEM((2 * size, CRASH_DEV), F32),
+            dma,
+            dma((2,)),
+            dma((2,)),
+            dma((CHUNKS,)),
+            dma((CHUNKS,)),
+            dma((n_dom,)),
+            dma((n_dom,)),
+            dma((CHUNKS, n_dom)),
+            dma((CHUNKS, n_dom)),
+        ],
+        compiler_params=pltpu.CompilerParams(
+            collective_id=0, has_side_effects=True, vmem_limit_bytes=48 * 1024 * 1024
+        ),
+    )(
+        leaf_hist, row(leaf_weight), row(leaf_parent), row(entry_parent), row(entry_dest), row(entry_crash),
+        row(entry_weight),
+    )
+
+
 def solution(mesh):
+    n_dom, n_sub = mesh.shape["dom"], mesh.shape["sub"]
+    aligned = n_dom & (n_dom - 1) == 0 and n_dom <= 8 and (4 * ENT_DEV // n_dom) % 128 == 0 and n_sub == 4
     in_specs = (
         P(None, ("dom", "sub")),
         P(("dom", "sub")),
@@ -77,5 +325,5 @@
     )
     out_specs = P(None, ("dom", "sub"))
     return jax.shard_map(
-        per_device, mesh=mesh, in_specs=in_specs, out_specs=out_specs, check_vma=False
-    )
+        fused if aligned else per_device, mesh=mesh, in_specs=in_specs, out_specs=out_specs, check_vma=False
+    )

time: 158 us -> 34.5 us (0.22)
  other arithmetic: 62.3 us -> 0 us
  local copies, waits for them, and re-layouts: 53.8 us -> 5.29 us
  Pallas kernels: 0 us -> 28.9 us
  starting transfers between devices: 17.2 us -> 0 us
  between operations: 14.3 us -> 0.02 us
  blocking collectives: 6.35 us -> 0 us
  waiting for transfers between devices: 3.61 us -> 0 us
    scatter-add x4 -> x0, other arithmetic: 52.6 us -> none  [the longest x1 14.7 us: per_device(): jax.ops.segment_sum(got_weight[0], got_crash[0], num_segments=CRASH_DEV)]
    gather x11 -> x0, local copies, waits for them, and re-layouts: 38.4 us -> none  [the longest x10 34.9 us: per_device(): jnp.searchsorted(sorted_destination, sorted_destination, side='left')]
    pallas_call x0 -> x1, Pallas kernels: none -> 28.9 us  [fused(): pl.pallas_call(functools.partial(fused_kernel, n_dom, capacity), out_shap...]
    all_to_all x3 -> x0, starting transfers between devices: 17.2 us -> none  [the longest x1 7.28 us: per_device(): lax.all_to_all(send_crash, 'dom', split_axis=1, concat_axis=1, tiled=True)]
    scatter x3 -> x0, local copies, waits for them, and re-layouts: 8.62 us -> none  [the longest x1 3.18 us: per_device(): jnp.zeros((1, slot_total), jnp.int32).at[0, slot_index].set(entry_crash)]
    unnamed x1 -> x0, blocking collectives: 6.35 us -> none
    sort x1 -> x0, other arithmetic: 3.77 us -> none  [per_device(): ordering = jnp.argsort(destination, stable=True)]
    all_to_all x3 -> x0, waiting for transfers between devices: 3.57 us -> none  [the longest x1 1.91 us: per_device(): lax.all_to_all(send_values, 'dom', split_axis=1, concat_axis=1, tiled=True)]
  transfers between devices with their start and end apart: 4 -> 0, of which waited for: 2 -> 0; matrix products, arithmetic and copies ran while one was open for 53% -> 0% of each run, Pallas kernels for 0% -> 0%
where the time goes in v1:
time: 34.5 us; the launch traced here: 34.2 us
  Pallas kernels  28.9 us (84%)
  local copies, waits for them, and re-layouts  5.29 us (15%)
    pallas_call x1, Pallas kernels, fused(): pl.pallas_call(functools.partial(fused_kernel, n_dom, capacity), out_shap...  28.9 us
    unnamed x15, local copies, waits for them, and re-layouts  5.29 us

profile of v1, /device:TPU:0, one launch (start us, length us, event | category | flops | bytes accessed | tf_op | source)
XLA Modules:
  0.0 34.2 jit_solution(17256459831078370812)
XLA Ops:
  0.0 0.0 copy-start.1
  0.0 0.0 copy-start.3
  0.0 0.7 %copy-done.1 = f32[2048]{0:T(1024)S(1)} copy-done((f32[2048]{0:T(1024)S(1)}, f32[2048]{0:T(1024)}, u32[]{:S(2)}) %copy-start.1) | copy-done | bytes 8216
  0.7 0.0 copy-done.3
  0.7 0.0 copy-start
  0.7 1.2 %copy-done = f32[112,2048]{1,0:T(8,128)S(1)} copy-done((f32[112,2048]{1,0:T(8,128)S(1)}, f32[112,2048]{1,0:T(8,128)}, u32[]{:S(2)}) %copy-start) | copy-done | bytes 917528
  1.9 0.0 copy-start.2
  1.9 0.7 %copy-done.2 = s32[2048]{0:T(1024)S(1)} copy-done((s32[2048]{0:T(1024)S(1)}, s32[2048]{0:T(1024)}, u32[]{:S(2)}) %copy-start.2) | copy-done | bytes 8216
  2.6 0.0 copy-start.4
  2.6 0.7 %copy-done.4 = s32[512,1]{0,1:T(1,128)S(1)} copy-done((s32[512,1]{0,1:T(1,128)S(1)}, s32[512,1]{0,1:T(1,128)}, u32[]{:S(2)}) %copy-start.4) | copy-done | bytes 2072
  3.3 0.0 copy-start.5
  3.3 0.7 %copy-done.5 = s32[512]{0:T(512)S(1)} copy-done((s32[512]{0:T(512)S(1)}, s32[512]{0:T(512)}, u32[]{:S(2)}) %copy-start.5) | copy-done | bytes 2072
  3.9 0.0 copy-start.6
  3.9 0.7 %copy-done.6 = f32[512]{0:T(512)S(1)} copy-done((f32[512]{0:T(512)S(1)}, f32[512]{0:T(512)}, u32[]{:S(2)}) %copy-start.6) | copy-done | bytes 2072
  4.6 28.9 %shard_map.73 = f32[80,512]{1,0:T(8,128)S(1)} custom-call(f32[112,2048]{1,0:T(8,128)S(1)} %copy-done, f32[1,2048]{1,0:T(1,128)S(1)} %bitcast.6, s32[1,2048]{1,0:T(1,128)S(1)} %bitcast.7, s32[1,512]{1,0:T(1,128)S(1)} %bitcast.8, s32[1,512]{1,0:T(1,128)S(1)} %bitcast.9, s32[1,512]{1,0:T(1,128)S(1)} %bitcast.10, f32[1,512]{1,0:T(1,128)S(1)} %bitcast.11), custom_call_target="tpu_custom_call" | custom-call | tf_op jit(solution)/shard_map/pallas_call | solution.py:275
  33.5 0.7 %copy.9 = f32[80,512]{1,0:T(8,128)} copy(f32[80,512]{1,0:T(8,128)S(1)} %shard_map.73) | data formatting | bytes 327680
Async XLA Ops:
  0.0 0.7 %copy-start.1 = (f32[2048]{0:T(1024)S(1)}, f32[2048]{0:T(1024)}, u32[]{:S(2)}) copy-start(f32[2048]{0:T(1024)} %param.8) | copy-start | bytes 24580
  0.0 0.7 %copy-start.3 = (s32[512]{0:T(512)S(1)}, s32[512]{0:T(512)}, u32[]{:S(2)}) copy-start(s32[512]{0:T(512)} %param.10) | copy-start | bytes 6148
  0.7 1.2 %copy-start = (f32[112,2048]{1,0:T(8,128)S(1)}, f32[112,2048]{1,0:T(8,128)}, u32[]{:S(2)}) copy-start(f32[112,2048]{1,0:T(8,128)} %hist_hbm.1) | copy-start | bytes 2752516
  1.9 0.7 %copy-start.2 = (s32[2048]{0:T(1024)S(1)}, s32[2048]{0:T(1024)}, u32[]{:S(2)}) copy-start(s32[2048]{0:T(1024)} %param.9) | copy-start | bytes 24580
  2.6 0.7 %copy-start.4 = (s32[512,1]{0,1:T(1,128)S(1)}, s32[512,1]{0,1:T(1,128)}, u32[]{:S(2)}) copy-start(s32[512,1]{0,1:T(1,128)} %param.11) | copy-start | bytes 6148
  3.3 0.7 %copy-start.5 = (s32[512]{0:T(512)S(1)}, s32[512]{0:T(512)}, u32[]{:S(2)}) copy-start(s32[512]{0:T(512)} %param.12) | copy-start | bytes 6148
  3.9 0.7 %copy-start.6 = (f32[512]{0:T(512)S(1)}, f32[512]{0:T(512)}, u32[]{:S(2)}) copy-start(f32[512]{0:T(512)} %param.13) | copy-start | bytes 6148

commit v2 on v1

--- a/solution.py
+++ b/solution.py
@@ -127,14 +127,24 @@
 
 def fused_kernel(
     n_dom, capacity,
-    hist_hbm, leaf_weight, leaf_parent, entry_parent, entry_dest, entry_crash, entry_weight,
+    hist_hbm, leaf_weight_hbm, leaf_parent_hbm, entry_parent_hbm, entry_dest_hbm, entry_crash_hbm, entry_weight_hbm,
     out_ref,
-    hist, data, kept, core_send, core_recv, x_send, x_recv, meta, meta_recv, pick, drop, pay, pay_recv, total,
-    hist_sem, core_ssem, core_rsem, x_ssem, x_rsem, meta_ssem, meta_rsem, pay_ssem, pay_rsem,
+    hist, leaf_weight, leaf_parent, entry_parent, entry_dest, entry_crash, entry_weight, data, kept, core_send, core_recv, x_send, x_recv, meta, meta_recv, pick, drop, pay, pay_recv, total,
+    load_sem, core_ssem, core_rsem, x_ssem, x_rsem, meta_ssem, meta_rsem, pay_ssem, pay_rsem,
 ):
     dom, sub = lax.axis_index("dom"), lax.axis_index("sub")
-    load = pltpu.make_async_copy(hist_hbm, hist, hist_sem)
-    load.start()
+    pairs = [
+        (leaf_parent_hbm, leaf_parent),
+        (hist_hbm, hist),
+        (leaf_weight_hbm, leaf_weight),
+        (entry_dest_hbm, entry_dest),
+        (entry_weight_hbm, entry_weight),
+        (entry_crash_hbm, entry_crash),
+        (entry_parent_hbm, entry_parent),
+    ]
+    loads = [pltpu.make_async_copy(source, target, load_sem.at[i]) for i, (source, target) in enumerate(pairs)]
+    for load in loads:
+        load.start()
     core = lax.rem(sub, 2)
     x = sub // 2
     core_peer = (dom, x * 2 + 1 - core)
@@ -159,7 +169,10 @@
             src_ref=source, dst_ref=target, send_sem=ssem, recv_sem=rsem, device_id=peer, device_id_type=MESH
         )
 
-    load.wait()
+    loads[0].wait()
+    first_hot = one_hot(leaf_parent[...] - ((1 - x) * 2 + 1 - core) * PAR_DEV, PAR_DEV)
+    loads[1].wait()
+    loads[2].wait()
     high = hist[...].astype(BF16)
     low = (hist[...] - high.astype(F32)).astype(BF16)
     table = remap_matrix()
@@ -180,7 +193,7 @@
     x_copies = [
         remote(x_send.at[span], x_recv.at[span], x_ssem.at[c], x_rsem.at[c], x_peer) for c, span in enumerate(spans)
     ]
-    core_send[0] = quarter((1 - x) * 2 + 1 - core)
+    core_send[0] = fold(dot_nt(data[...], first_hot), 2)
     pl.semaphore_wait(barrier, n_dom + 1)
     core_copies[0].start()
     kept[0] = quarter((1 - x) * 2 + core)
@@ -192,6 +205,8 @@
     core_copies[1].start()
     kept[1] = quarter(x * 2 + core)
 
+    for load in loads[3:]:
+        load.wait()
     entries = entry_parent.shape[1]
     named = entry_dest[...]
     mask = jnp.zeros_like(named)
@@ -275,10 +290,16 @@
     return pl.pallas_call(
         functools.partial(fused_kernel, n_dom, capacity),
         out_shape=jax.ShapeDtypeStruct((ROWS, CRASH_DEV), F32),
-        in_specs=[pl.BlockSpec(memory_space=pl.ANY)] + [vmem] * 6,
+        in_specs=[pl.BlockSpec(memory_space=pltpu.HBM)] * 7,
         out_specs=vmem,
         scratch_shapes=[
             pltpu.VMEM((HIST * THICK, leaves), F32),
+            pltpu.VMEM((1, leaves), F32),
+            pltpu.VMEM((1, leaves), I32),
+            pltpu.VMEM((1, ENT_DEV), I32),
+            pltpu.VMEM((1, ENT_DEV), I32),
+            pltpu.VMEM((1, ENT_DEV), I32),
+            pltpu.VMEM((1, ENT_DEV), F32),
             pltpu.VMEM((2 * (HEAD + ROWS), leaves), BF16),
             pltpu.VMEM((2, HEAD + ROWS, PAR_DEV), F32),
             pltpu.VMEM((2, HEAD + ROWS, PAR_DEV), F32),
@@ -292,7 +313,7 @@
             pltpu.VMEM((CHUNKS, n_dom, size, capacity), F32),
             pltpu.VMEM((CHUNKS, n_dom, size, capacity), F32),
             pltpu.VMEM((2 * size, CRASH_DEV), F32),
-            dma,
+            dma((7,)),
             dma((2,)),
             dma((2,)),
             dma((CHUNKS,)),
@@ -303,7 +324,7 @@
             dma((CHUNKS, n_dom)),
         ],
         compiler_params=pltpu.CompilerParams(
-            collective_id=0, has_side_effects=True, vmem_limit_bytes=48 * 1024 * 1024
+            collective_id=0, has_side_effects=True, vmem_limit_bytes=60 * 1024 * 1024
         ),
     )(
         leaf_hist, row(leaf_weight), row(leaf_parent), row(entry_parent), row(entry_dest), row(entry_crash),

time: 34.5 us -> 31.4 us (0.910)
  local copies, waits for them, and re-layouts: 5.29 us -> 1.59 us
  Pallas kernels: 28.9 us -> 29.6 us
    unnamed x15 -> x1, local copies, waits for them, and re-layouts: 5.29 us -> 1.59 us
    pallas_call x1, Pallas kernels: 28.9 us -> 29.6 us  [fused(): pl.pallas_call(functools.partial(fused_kernel, n_dom, capacity), out_shap...]
where the time goes in v2:
time: 31.4 us; the launch traced here: 31.2 us
  Pallas kernels  29.6 us (94%)
  local copies, waits for them, and re-layouts  1.59 us (5%)
    pallas_call x1, Pallas kernels, fused(): pl.pallas_call(functools.partial(fused_kernel, n_dom, capacity), out_shap...  29.6 us
    unnamed x1, local copies, waits for them, and re-layouts  1.59 us

profile of v2, /device:TPU:0, one launch (start us, length us, event | category | flops | bytes accessed | tf_op | source)
XLA Modules:
  0.0 31.2 jit_solution(16695486992340471121)
XLA Ops:
  0.0 29.6 %shard_map.73 = f32[80,512]{1,0:T(8,128)} custom-call(f32[112,2048]{1,0:T(8,128)} %hist_hbm.1, f32[1,2048]{1,0:T(1,128)} %bitcast.6, s32[1,2048]{1,0:T(1,128)} %bitcast.7, s32[1,512]{1,0:T(1,128)} %bitcast.8, s32[1,512]{1,0:T(1,128)} %bitcast.9, s32[1,512]{1,0:T(1,128)} %bitcast.10, f32[1,512]{1,0:T(1,128)} %bitcast.11), custom_call_target="tpu_custom_call" | custom-call | tf_op jit(solution)/shard_map/pallas_call | solution.py:290
  29.6 1.6 %copy.9 = f32[80,512]{1,0:T(8,128)} copy(f32[80,512]{1,0:T(8,128)} %shard_map.73) | data formatting | bytes 327680

commit v3 on v2

--- a/solution.py
+++ b/solution.py
@@ -289,7 +289,7 @@
     row = lambda array: array.reshape(1, -1)
     return pl.pallas_call(
         functools.partial(fused_kernel, n_dom, capacity),
-        out_shape=jax.ShapeDtypeStruct((ROWS, CRASH_DEV), F32),
+        out_shape=pltpu.VMEM((ROWS, CRASH_DEV), F32),
         in_specs=[pl.BlockSpec(memory_space=pltpu.HBM)] * 7,
         out_specs=vmem,
         scratch_shapes=[

time: 31.4 us -> 29.9 us (0.952)
  local copies, waits for them, and re-layouts: 1.59 us -> 0.67 us
  Pallas kernels: 29.6 us -> 29 us
    unnamed x1, local copies, waits for them, and re-layouts: 1.59 us -> 0.67 us
    pallas_call x1, Pallas kernels: 29.6 us -> 29 us  [fused(): pl.pallas_call(functools.partial(fused_kernel, n_dom, capacity), out_shap...]
where the time goes in v3:
time: 29.9 us; the launch traced here: 29.7 us
  Pallas kernels  29 us (97%)
  local copies, waits for them, and re-layouts  0.67 us (2%)
    pallas_call x1, Pallas kernels, fused(): pl.pallas_call(functools.partial(fused_kernel, n_dom, capacity), out_shap...  29 us
    unnamed x1, local copies, waits for them, and re-layouts  0.67 us

profile of v3, /device:TPU:0, one launch (start us, length us, event | category | flops | bytes accessed | tf_op | source)
XLA Modules:
  0.0 29.7 jit_solution(10104079769756008678)
XLA Ops:
  0.0 29.0 %shard_map.73 = f32[80,512]{1,0:T(8,128)S(1)} custom-call(f32[112,2048]{1,0:T(8,128)} %hist_hbm.1, f32[1,2048]{1,0:T(1,128)} %bitcast.6, s32[1,2048]{1,0:T(1,128)} %bitcast.7, s32[1,512]{1,0:T(1,128)} %bitcast.8, s32[1,512]{1,0:T(1,128)} %bitcast.9, s32[1,512]{1,0:T(1,128)} %bitcast.10, f32[1,512]{1,0:T(1,128)} %bitcast.11), custom_call_target="tpu_custom_call" | custom-call | tf_op jit(solution)/shard_map/pallas_call | solution.py:290
  29.0 0.7 %copy.9 = f32[80,512]{1,0:T(8,128)} copy(f32[80,512]{1,0:T(8,128)S(1)} %shard_map.73) | data formatting | bytes 327680

commit v4 on v3

--- a/solution.py
+++ b/solution.py
@@ -73,7 +73,8 @@
 F32, BF16, I32 = jnp.float32, jnp.bfloat16, jnp.int32
 HEAD = 8
 ROWS = HIST * CTHICK
-CHUNKS = 2
+SIZES = (16, 64)
+CHUNKS = len(SIZES)
 
 
 def dot_nn(a, b):
@@ -129,7 +130,7 @@
     n_dom, capacity,
     hist_hbm, leaf_weight_hbm, leaf_parent_hbm, entry_parent_hbm, entry_dest_hbm, entry_crash_hbm, entry_weight_hbm,
     out_ref,
-    hist, leaf_weight, leaf_parent, entry_parent, entry_dest, entry_crash, entry_weight, data, kept, core_send, core_recv, x_send, x_recv, meta, meta_recv, pick, drop, pay, pay_recv, total,
+    hist, leaf_weight, leaf_parent, entry_parent, entry_dest, entry_crash, entry_weight, data, kept, core_send, core_recv, x_send, x_recv, meta, meta_recv, pick, drop, pay, pay_recv,
     load_sem, core_ssem, core_rsem, x_ssem, x_rsem, meta_ssem, meta_rsem, pay_ssem, pay_rsem,
 ):
     dom, sub = lax.axis_index("dom"), lax.axis_index("sub")
@@ -188,7 +189,8 @@
     core_copies = [
         remote(core_send.at[i], core_recv.at[i], core_ssem.at[i], core_rsem.at[i], core_peer) for i in range(2)
     ]
-    bounds = [0] + [HEAD + ROWS * (c + 1) // CHUNKS for c in range(CHUNKS)]
+    bounds = [0] + [HEAD + sum(SIZES[: c + 1]) for c in range(CHUNKS)]
+    places = [pl.ds(sum(SIZES[:c]), SIZES[c]) for c in range(CHUNKS)]
     spans = [pl.ds(bounds[c], bounds[c + 1] - bounds[c]) for c in range(CHUNKS)]
     x_copies = [
         remote(x_send.at[span], x_recv.at[span], x_ssem.at[c], x_rsem.at[c], x_peer) for c, span in enumerate(spans)
@@ -254,9 +256,9 @@
             sums = sums[HEAD:]
         means = terms(sums * inverse, 2)
         for m in list(range(n_dom - 1, -1, -1)):
-            pay[c, m] = fold(dot_nn(means, pick[m]), 2) * meta[m, :1]
+            pay[m, places[c]] = fold(dot_nn(means, pick[m]), 2) * meta[m, :1]
             if m:
-                copy = remote(pay.at[c, m], pay_recv.at[c, m], pay_ssem.at[c, m], pay_rsem.at[c, m], dom_peers[m])
+                copy = remote(pay.at[m, places[c]], pay_recv.at[m, places[c]], pay_ssem.at[c, m], pay_rsem.at[c, m], dom_peers[m])
                 copy.start()
                 pay_copies[c, m] = copy
 
@@ -268,13 +270,12 @@
         drop[m] = one_hot(got[1:2].astype(I32), CRASH_DEV)
         crash_weight = crash_weight + fold(dot_nt(terms(got, 3), drop[m]), 3)[:1]
     inverse = 1.0 / jnp.maximum(crash_weight, 1.0)
-    size = ROWS // CHUNKS
     for c in range(CHUNKS):
-        total[...] = dot_nt(terms(pay[c, 0], 2), drop[0])
-        for m in list(range(n_dom - 1, 0, -1)):
+        total = dot_nt(terms(pay[0, places[c]], 2), drop[0])
+        for m in list(range(1, n_dom // 2)) + list(range(n_dom - 1, n_dom // 2 - 1, -1)):
             pay_copies[c, m].wait_recv()
-            total[...] += dot_nt(terms(pay_recv[c, m], 2), drop[m])
-        out_ref[pl.ds(c * size, size)] = fold(total[...], 2) * inverse
+            total += dot_nt(terms(pay_recv[m, places[c]], 2), drop[m])
+        out_ref[places[c]] = fold(total, 2) * inverse
     for copy in core_copies + x_copies + list(meta_copies.values()) + list(pay_copies.values()):
         copy.wait_send()
 
@@ -283,7 +284,6 @@
     n_dom = lax.axis_size("dom")
     capacity = 4 * ENT_DEV // n_dom
     leaves = leaf_hist.shape[1]
-    size = ROWS // CHUNKS
     vmem = pl.BlockSpec(memory_space=pltpu.VMEM)
     dma = pltpu.SemaphoreType.DMA
     row = lambda array: array.reshape(1, -1)
@@ -310,9 +310,8 @@
             pltpu.VMEM((n_dom, 8, capacity), F32),
             pltpu.VMEM((n_dom, PAR_DEV, capacity), BF16),
             pltpu.VMEM((n_dom, CRASH_DEV, capacity), BF16),
-            pltpu.VMEM((CHUNKS, n_dom, size, capacity), F32),
-            pltpu.VMEM((CHUNKS, n_dom, size, capacity), F32),
-            pltpu.VMEM((2 * size, CRASH_DEV), F32),
+            pltpu.VMEM((n_dom, ROWS, capacity), F32),
+            pltpu.VMEM((n_dom, ROWS, capacity), F32),
             dma((7,)),
             dma((2,)),
             dma((2,)),

time: 29.9 us -> 28.9 us (0.967)
  Pallas kernels: 29 us -> 28 us
    pallas_call x1, Pallas kernels: 29 us -> 28 us  [fused(): pl.pallas_call(functools.partial(fused_kernel, n_dom, capacity), out_shap...]
where the time goes in v4:
time: 28.9 us; the launch traced here: 28.7 us
  Pallas kernels  28 us (97%)
  local copies, waits for them, and re-layouts  0.67 us (2%)
    pallas_call x1, Pallas kernels, fused(): pl.pallas_call(functools.partial(fused_kernel, n_dom, capacity), out_shap...  28 us
    unnamed x1, local copies, waits for them, and re-layouts  0.67 us

profile of v4, /device:TPU:0, one launch (start us, length us, event | category | flops | bytes accessed | tf_op | source)
XLA Modules:
  0.0 28.7 jit_solution(10748072271333470157)
XLA Ops:
  0.0 28.0 %shard_map.73 = f32[80,512]{1,0:T(8,128)S(1)} custom-call(f32[112,2048]{1,0:T(8,128)} %hist_hbm.1, f32[1,2048]{1,0:T(1,128)} %bitcast.6, s32[1,2048]{1,0:T(1,128)} %bitcast.7, s32[1,512]{1,0:T(1,128)} %bitcast.8, s32[1,512]{1,0:T(1,128)} %bitcast.9, s32[1,512]{1,0:T(1,128)} %bitcast.10, f32[1,512]{1,0:T(1,128)} %bitcast.11), custom_call_target="tpu_custom_call" | custom-call | tf_op jit(solution)/shard_map/pallas_call | solution.py:290
  28.0 0.7 %copy.9 = f32[80,512]{1,0:T(8,128)} copy(f32[80,512]{1,0:T(8,128)S(1)} %shard_map.73) | data formatting | bytes 327680
